TPU v7x, 32 devices: a whole 2x2x4 slice. The times are simulated.
32 devices in a mesh: tm: 2 (over core), space: 16 (over z, y, x).
Axes of the slice: x: 2, y: 2, z: 4, core: 2. Of those that a mesh axis runs over, the one named last changes fastest.
Arguments:
- initial_guess: float32 [2, 4, 32, 64, 256], P('tm', None, 'space'), may hold values from -6 to 6
- viscosity: float32 [32, 64, 256], P('space'), may hold values from 0.03 to 0.15
Outputs:
- end_states: float32 [2, 4, 32, 64, 256], P('tm', None, 'space')
All inputs are finite; a program needn't handle non-finite values.
Results may differ from a plain program's by a relative error of at most 0.00002.
Values sent between devices are 32-bit elements; how exact they have to be, the bound alone decides.
A program may use at most 64 MiB of HBM per device.

v0:
```python
import jax
import jax.numpy as jnp
from jax import lax
from jax.sharding import PartitionSpec as P

ITERS = 2


time_step = 0.4
tension = 0.1
level_diffusion = 0.02
shear_rate = 1.0


def padded_2(value, sides, width):
    for axis, dim in sides:
        peers, length = (lax.axis_size(axis), value.shape[dim])
        up = [(i, (i + 1) % peers) for i in range(peers)]
        down = [(j, i) for i, j in up]
        last = lax.slice_in_dim(value, length - width, length, axis=dim)
        first = lax.slice_in_dim(value, 0, width, axis=dim)
        before = lax.ppermute(last, axis, up)
        after = lax.ppermute(first, axis, down)
        value = jnp.concatenate([before, value, after], axis=dim)
    return value


def passed_along(value, axis, by):
    peers = lax.axis_size(axis)
    pairs = [(i, i + by) for i in range(peers) if 0 <= i + by < peers]
    return lax.ppermute(value, axis, pairs)


def tendency(center, east_side, west_side, viscosity, shear_speed):
    north_side = jnp.roll(center, -1, axis=2)
    south_side = jnp.roll(center, 1, axis=2)
    padded = jnp.pad(center, ((0, 0), (0, 0), (0, 0), (1, 1)))
    top_side = padded[..., 2:]
    bottom_side = padded[..., :-2]
    grad_x = 0.5 * (east_side - west_side)
    grad_y = 0.5 * (north_side - south_side)
    grad_z = 0.5 * (top_side - bottom_side)
    laplace = (
        east_side + west_side + north_side + south_side + top_side + bottom_side - 6.0 * center
    )
    stream_speed = center[0] + shear_speed
    advect = -(stream_speed * grad_x + center[1] * grad_y + center[2] * grad_z)
    curvature = tension * laplace[3]
    momentum = (
        advect[:3]
        + viscosity * laplace[:3]
        + curvature * jnp.stack([grad_x[3], grad_y[3], grad_z[3]])
    )
    level_set = advect[3:] + level_diffusion * laplace[3:]
    return jnp.concatenate([momentum, level_set], axis=0)


def extend(field):
    return padded_2(field, (("space", 1),), 1)


def sdc_sweep(start_ext, old_tends, viscosity, shear_speed):

    def evaluate(ext):
        return tendency(ext[:, 1:-1], ext[:, 2:], ext[:, :-2], viscosity, shear_speed)

    old_zero, old_one, old_two = old_tends
    node_zero = start_ext[:, 1:-1]
    tend_zero = evaluate(start_ext)
    node_one = (
        node_zero
        + 0.5 * time_step * (tend_zero - old_zero)
        + time_step * (5.0 / 24.0 * old_zero + 1.0 / 3.0 * old_one - 1.0 / 24.0 * old_two)
    )
    tend_one = evaluate(extend(node_one))
    node_two = (
        node_one
        + 0.5 * time_step * (tend_one - old_one)
        + time_step * (-1.0 / 24.0 * old_zero + 1.0 / 3.0 * old_one + 5.0 / 24.0 * old_two)
    )
    ext_two = extend(node_two)
    tend_two = evaluate(ext_two)
    return (node_two, (tend_zero, tend_one, tend_two), ext_two)


def on_device(initial_guess, viscosity):
    state_now = initial_guess[0]
    depth = state_now.shape[3]
    shear_speed = shear_rate * (lax.iota(jnp.float32, depth) + 0.5) / depth
    is_first = lax.axis_index("tm") == 0
    guess_ext = extend(state_now)
    first_tendency = tendency(
        guess_ext[:, 1:-1], guess_ext[:, 2:], guess_ext[:, :-2], viscosity, shear_speed
    )
    old_tends = (first_tendency, first_tendency, first_tendency)
    end_value = state_now
    for iteration in range(ITERS):
        received = passed_along(end_value, "tm", 1)
        start_value = jnp.where(is_first, state_now, received)
        end_value, old_tends, end_ext = sdc_sweep(
            extend(start_value), old_tends, viscosity, shear_speed
        )
    return end_value[None]


def solution(mesh):
    placed = (P("tm", None, "space", None, None), P("space", None, None))
    return jax.shard_map(
        on_device,
        mesh=mesh,
        in_specs=placed,
        out_specs=P("tm", None, "space", None, None),
        check_vma=False,
    )
```

profile of v0, /device:TPU:0, one launch (start us, length us, event | category | flops | bytes accessed | tf_op | source)
XLA Modules:
  0.0 95.5 jit_solution(9303329098083984251)
XLA Ops:
  0.0 2.5 %collective-permute-start = (f32[4,2,64,256]{3,2,1,0:T(8,128)}, f32[4,2,64,256]{3,2,1,0:T(8,128)S(1)}, u32[]{:S(2)}, u32[]{:S(2)}) collective-permute-start(f32[4,2,64,256]{3,2,1,0:T(8,128)} %bitcast.55), channel_id=1, source_target_pairs={{0,16},{1,17},{2,18},{3,19},{4,20},{5,21},{6,22},{7,23},{8,24},{9,... | collective-permute-start | bytes 1572872 | tf_op jit(solution)/shard_map/ppermute | solution.py:31
  2.5 1.1 %fusion.93 = (f32[4,1,64,256]{3,2,1,0:T(8,128)S(1)}, f32[4,1,64,256]{3,2,1,0:T(8,128)S(1)}) fusion(f32[4,2,64,256]{3,2,1,0:T(8,128)} %bitcast.56), kind=kLoop, calls=%fused_computation.194 | loop fusion | bytes 1048576 | tf_op jit(solution)/shard_map/slice | solution.py:21
  3.6 6.4 %collective-permute-start.3 = (f32[4,1,64,256]{3,2,1,0:T(8,128)S(1)}, f32[4,1,64,256]{3,2,1,0:T(8,128)S(1)}, u32[]{:S(2)}, u32[]{:S(2)}) collective-permute-start(f32[4,1,64,256]{3,2,1,0:T(8,128)S(1)} %get-tuple-element.90), channel_id=1, source_target_pairs={{1,0},{2,1},{3,2},{4,3},{5,4},{6,5},{7,6},{8,7},{9,8},{10,9},{11,1... | collective-permute-start | bytes 786440 | tf_op jit(solution)/shard_map/ppermute | solution.py:23
  10.2 4.9 %collective-permute-done.3 = f32[4,1,64,256]{3,2,1,0:T(8,128)S(1)} collective-permute-done((f32[4,1,64,256]{3,2,1,0:T(8,128)S(1)}, f32[4,1,64,256]{3,2,1,0:T(8,128)S(1)}, u32[]{:S(2)}, u32[]{:S(2)}) %collective-permute-start.3) | collective-permute-done | bytes 262176 | tf_op jit(solution)/shard_map/ppermute | solution.py:23
  15.1 5.8 %collective-permute-done.4 = f32[4,1,64,256]{3,2,1,0:T(8,128)S(1)} collective-permute-done((f32[4,1,64,256]{3,2,1,0:T(8,128)S(1)}, f32[4,1,64,256]{3,2,1,0:T(8,128)S(1)}, u32[]{:S(2)}, u32[]{:S(2)}) %collective-permute-start.4) | collective-permute-done | bytes 262176 | tf_op jit(solution)/shard_map/ppermute | solution.py:22
  20.9 0.4 add_negate_fusion.4
  21.3 0.4 multiply_subtract_fusion.4
  22.0 2.3 %collective-permute-start.1 = (f32[4,1,64,256]{3,2,1,0:T(8,128)S(1)}, f32[4,1,64,256]{3,2,1,0:T(8,128)S(1)}, u32[]{:S(2)}, u32[]{:S(2)}) collective-permute-start(f32[4,1,64,256]{3,2,1,0:T(8,128)S(1)} %get-tuple-element.79), channel_id=1, source_target_pairs={{1,0},{2,1},{3,2},{4,3},{5,4},{6,5},{7,6},{8,7},{9,8},{10,9},{11,1... | collective-permute-start | bytes 786440 | tf_op jit(solution)/shard_map/ppermute | solution.py:23
  24.4 6.9 %collective-permute-done.1 = f32[4,1,64,256]{3,2,1,0:T(8,128)S(1)} collective-permute-done((f32[4,1,64,256]{3,2,1,0:T(8,128)S(1)}, f32[4,1,64,256]{3,2,1,0:T(8,128)S(1)}, u32[]{:S(2)}, u32[]{:S(2)}) %collective-permute-start.1) | collective-permute-done | bytes 262176 | tf_op jit(solution)/shard_map/ppermute | solution.py:23
  31.3 3.0 %collective-permute-done.2 = f32[4,1,64,256]{3,2,1,0:T(8,128)S(1)} collective-permute-done((f32[4,1,64,256]{3,2,1,0:T(8,128)S(1)}, f32[4,1,64,256]{3,2,1,0:T(8,128)S(1)}, u32[]{:S(2)}, u32[]{:S(2)}) %collective-permute-start.2) | collective-permute-done | bytes 262176 | tf_op jit(solution)/shard_map/ppermute | solution.py:22
  34.3 0.5 add_negate_fusion.5
  34.8 0.4 multiply_subtract_fusion.5
  35.3 0.9 copy-done.1
  36.6 3.2 %collective-permute-start.5 = (f32[4,1,64,256]{3,2,1,0:T(8,128)S(1)}, f32[4,1,64,256]{3,2,1,0:T(8,128)S(1)}, u32[]{:S(2)}, u32[]{:S(2)}) collective-permute-start(f32[4,1,64,256]{3,2,1,0:T(8,128)S(1)} %get-tuple-element.68), channel_id=1, source_target_pairs={{1,0},{2,1},{3,2},{4,3},{5,4},{6,5},{7,6},{8,7},{9,8},{10,9},{11,1... | collective-permute-start | bytes 786440 | tf_op jit(solution)/shard_map/ppermute | solution.py:23
  39.9 6.0 %collective-permute-done.5 = f32[4,1,64,256]{3,2,1,0:T(8,128)S(1)} collective-permute-done((f32[4,1,64,256]{3,2,1,0:T(8,128)S(1)}, f32[4,1,64,256]{3,2,1,0:T(8,128)S(1)}, u32[]{:S(2)}, u32[]{:S(2)}) %collective-permute-start.5) | collective-permute-done | bytes 262176 | tf_op jit(solution)/shard_map/ppermute | solution.py:23
  45.9 4.0 %collective-permute-done.6 = f32[4,1,64,256]{3,2,1,0:T(8,128)S(1)} collective-permute-done((f32[4,1,64,256]{3,2,1,0:T(8,128)S(1)}, f32[4,1,64,256]{3,2,1,0:T(8,128)S(1)}, u32[]{:S(2)}, u32[]{:S(2)}) %collective-permute-start.6) | collective-permute-done | bytes 262176 | tf_op jit(solution)/shard_map/ppermute | solution.py:22
  49.9 0.5 add_negate_fusion.3
  51.2 1.3 %collective-permute-start.7 = (f32[4,2,64,256]{3,2,1,0:T(8,128)S(1)}, f32[4,2,64,256]{3,2,1,0:T(8,128)S(1)}, u32[]{:S(2)}, u32[]{:S(2)}) collective-permute-start(f32[4,2,64,256]{3,2,1,0:T(8,128)S(1)} %multiply_add_fusion), channel_id=1, source_target_pairs={{0,16},{1,17},{2,18},{3,19},{4,20},{5,21},{6,22},{7,23},{8,24},{9,... | collective-permute-start | bytes 1572872 | tf_op jit(solution)/shard_map/ppermute | solution.py:31
  52.6 1.4 %collective-permute-start.10 = (f32[4,1,64,256]{3,2,1,0:T(8,128)S(1)}, f32[4,1,64,256]{3,2,1,0:T(8,128)S(1)}, u32[]{:S(2)}, u32[]{:S(2)}) collective-permute-start(f32[4,1,64,256]{3,2,1,0:T(8,128)S(1)} %get-tuple-element.46), channel_id=1, source_target_pairs={{1,0},{2,1},{3,2},{4,3},{5,4},{6,5},{7,6},{8,7},{9,8},{10,9},{11,1... | collective-permute-start | bytes 786440 | tf_op jit(solution)/shard_map/ppermute | solution.py:23
  54.0 0.7 collective-permute-start.11
  54.8 6.2 %collective-permute-done.10 = f32[4,1,64,256]{3,2,1,0:T(8,128)S(1)} collective-permute-done((f32[4,1,64,256]{3,2,1,0:T(8,128)S(1)}, f32[4,1,64,256]{3,2,1,0:T(8,128)S(1)}, u32[]{:S(2)}, u32[]{:S(2)}) %collective-permute-start.10) | collective-permute-done | bytes 262176 | tf_op jit(solution)/shard_map/ppermute | solution.py:23
  61.0 3.1 %collective-permute-done.11 = f32[4,1,64,256]{3,2,1,0:T(8,128)S(1)} collective-permute-done((f32[4,1,64,256]{3,2,1,0:T(8,128)S(1)}, f32[4,1,64,256]{3,2,1,0:T(8,128)S(1)}, u32[]{:S(2)}, u32[]{:S(2)}) %collective-permute-start.11) | collective-permute-done | bytes 262176 | tf_op jit(solution)/shard_map/ppermute | solution.py:22
  64.7 0.5 add_negate_fusion.1
  65.3 3.7 %collective-permute-start.8 = (f32[4,1,64,256]{3,2,1,0:T(8,128)S(1)}, f32[4,1,64,256]{3,2,1,0:T(8,128)S(1)}, u32[]{:S(2)}, u32[]{:S(2)}) collective-permute-start(f32[4,1,64,256]{3,2,1,0:T(8,128)S(1)} %get-tuple-element.57), channel_id=1, source_target_pairs={{1,0},{2,1},{3,2},{4,3},{5,4},{6,5},{7,6},{8,7},{9,8},{10,9},{11,1... | collective-permute-start | bytes 786440 | tf_op jit(solution)/shard_map/ppermute | solution.py:23
  69.1 4.5 %collective-permute-done.8 = f32[4,1,64,256]{3,2,1,0:T(8,128)S(1)} collective-permute-done((f32[4,1,64,256]{3,2,1,0:T(8,128)S(1)}, f32[4,1,64,256]{3,2,1,0:T(8,128)S(1)}, u32[]{:S(2)}, u32[]{:S(2)}) %collective-permute-start.8) | collective-permute-done | bytes 262176 | tf_op jit(solution)/shard_map/ppermute | solution.py:23
  73.5 5.5 %collective-permute-done.9 = f32[4,1,64,256]{3,2,1,0:T(8,128)S(1)} collective-permute-done((f32[4,1,64,256]{3,2,1,0:T(8,128)S(1)}, f32[4,1,64,256]{3,2,1,0:T(8,128)S(1)}, u32[]{:S(2)}, u32[]{:S(2)}) %collective-permute-start.9) | collective-permute-done | bytes 262176 | tf_op jit(solution)/shard_map/ppermute | solution.py:22
  79.0 0.5 add_negate_fusion.2
  80.6 2.8 %collective-permute-start.12 = (f32[4,1,64,256]{3,2,1,0:T(8,128)S(1)}, f32[4,1,64,256]{3,2,1,0:T(8,128)S(1)}, u32[]{:S(2)}, u32[]{:S(2)}) collective-permute-start(f32[4,1,64,256]{3,2,1,0:T(8,128)S(1)} %get-tuple-element.35), channel_id=1, source_target_pairs={{1,0},{2,1},{3,2},{4,3},{5,4},{6,5},{7,6},{8,7},{9,8},{10,9},{11,1... | collective-permute-start | bytes 786440 | tf_op jit(solution)/shard_map/ppermute | solution.py:23
  83.5 5.9 %collective-permute-done.12 = f32[4,1,64,256]{3,2,1,0:T(8,128)S(1)} collective-permute-done((f32[4,1,64,256]{3,2,1,0:T(8,128)S(1)}, f32[4,1,64,256]{3,2,1,0:T(8,128)S(1)}, u32[]{:S(2)}, u32[]{:S(2)}) %collective-permute-start.12) | collective-permute-done | bytes 262176 | tf_op jit(solution)/shard_map/ppermute | solution.py:23
  89.4 4.0 %collective-permute-done.13 = f32[4,1,64,256]{3,2,1,0:T(8,128)S(1)} collective-permute-done((f32[4,1,64,256]{3,2,1,0:T(8,128)S(1)}, f32[4,1,64,256]{3,2,1,0:T(8,128)S(1)}, u32[]{:S(2)}, u32[]{:S(2)}) %collective-permute-start.13) | collective-permute-done | bytes 262176 | tf_op jit(solution)/shard_map/ppermute | solution.py:22
  93.3 0.5 add_negate_fusion
  94.5 1.0 %fusion.6 = f32[1,4,2,64,256]{4,3,2,1,0:T(8,128)} fusion(f32[4,2,64,256]{3,2,1,0:T(8,128)S(1)} %fusion.2, f32[1,2,64,256]{3,2,1,0:T(8,128)S(1)} %get-tuple-element.30, f32[3,2,64,256]{3,2,1,0:T(8,128)S(1)} %fusion.20, f32[1,2,64,256]{3,2,1,0:T(8,128)S(1)} %get-tuple-element.41, f32[3,2,64,256]{3,2,1,0:T(8,128)S(1)} %get-tuple-element.94, ...), kind=kLoop, calls=%fused_computation.48 | loop fusion | flops 1835008 | bytes 3145728 | tf_op jit(solution)/shard_map/broadcast_in_dim | solution.py:103
  (67 shorter events, 4.3 us)
Async XLA Ops:
  0.0 10.0 %copy-start = (f32[1,4,2,64,256]{4,3,2,1,0:T(8,128)S(1)}, f32[1,4,2,64,256]{4,3,2,1,0:T(8,128)}, u32[]{:S(2)}) copy-start(f32[1,4,2,64,256]{4,3,2,1,0:T(8,128)} %param.2) | copy-start | bytes 1572868
  0.0 21.8 %collective-permute-start = (f32[4,2,64,256]{3,2,1,0:T(8,128)}, f32[4,2,64,256]{3,2,1,0:T(8,128)S(1)}, u32[]{:S(2)}, u32[]{:S(2)}) collective-permute-start(f32[4,2,64,256]{3,2,1,0:T(8,128)} %bitcast.55), channel_id=1, source_target_pairs={{0,16},{1,17},{2,18},{3,19},{4,20},{5,21},{6,22},{7,23},{8,24},{9,... | collective-permute-start | bytes 1572872 | tf_op jit(solution)/shard_map/ppermute | solution.py:31
  3.6 11.5 %collective-permute-start.3 = (f32[4,1,64,256]{3,2,1,0:T(8,128)S(1)}, f32[4,1,64,256]{3,2,1,0:T(8,128)S(1)}, u32[]{:S(2)}, u32[]{:S(2)}) collective-permute-start(f32[4,1,64,256]{3,2,1,0:T(8,128)S(1)} %get-tuple-element.90), channel_id=1, source_target_pairs={{1,0},{2,1},{3,2},{4,3},{5,4},{6,5},{7,6},{8,7},{9,8},{10,9},{11,1... | collective-permute-start | bytes 786440 | tf_op jit(solution)/shard_map/ppermute | solution.py:23
  10.0 10.9 %collective-permute-start.4 = (f32[4,1,64,256]{3,2,1,0:T(8,128)S(1)}, f32[4,1,64,256]{3,2,1,0:T(8,128)S(1)}, u32[]{:S(2)}, u32[]{:S(2)}) collective-permute-start(f32[4,1,64,256]{3,2,1,0:T(8,128)S(1)} %get-tuple-element.91), channel_id=1, source_target_pairs={{0,1},{1,2},{2,3},{3,4},{4,5},{5,6},{6,7},{7,8},{8,9},{9,10},{10,1... | collective-permute-start | bytes 786440 | tf_op jit(solution)/shard_map/ppermute | solution.py:22
  22.0 9.3 %collective-permute-start.1 = (f32[4,1,64,256]{3,2,1,0:T(8,128)S(1)}, f32[4,1,64,256]{3,2,1,0:T(8,128)S(1)}, u32[]{:S(2)}, u32[]{:S(2)}) collective-permute-start(f32[4,1,64,256]{3,2,1,0:T(8,128)S(1)} %get-tuple-element.79), channel_id=1, source_target_pairs={{1,0},{2,1},{3,2},{4,3},{5,4},{6,5},{7,6},{8,7},{9,8},{10,9},{11,1... | collective-permute-start | bytes 786440 | tf_op jit(solution)/shard_map/ppermute | solution.py:23
  24.3 10.0 %collective-permute-start.2 = (f32[4,1,64,256]{3,2,1,0:T(8,128)S(1)}, f32[4,1,64,256]{3,2,1,0:T(8,128)S(1)}, u32[]{:S(2)}, u32[]{:S(2)}) collective-permute-start(f32[4,1,64,256]{3,2,1,0:T(8,128)S(1)} %get-tuple-element.80), channel_id=1, source_target_pairs={{0,1},{1,2},{2,3},{3,4},{4,5},{5,6},{6,7},{7,8},{8,9},{9,10},{10,1... | collective-permute-start | bytes 786440 | tf_op jit(solution)/shard_map/ppermute | solution.py:22
  35.2 0.9 copy-start.1
  36.6 9.3 %collective-permute-start.5 = (f32[4,1,64,256]{3,2,1,0:T(8,128)S(1)}, f32[4,1,64,256]{3,2,1,0:T(8,128)S(1)}, u32[]{:S(2)}, u32[]{:S(2)}) collective-permute-start(f32[4,1,64,256]{3,2,1,0:T(8,128)S(1)} %get-tuple-element.68), channel_id=1, source_target_pairs={{1,0},{2,1},{3,2},{4,3},{5,4},{6,5},{7,6},{8,7},{9,8},{10,9},{11,1... | collective-permute-start | bytes 786440 | tf_op jit(solution)/shard_map/ppermute | solution.py:23
  39.8 10.1 %collective-permute-start.6 = (f32[4,1,64,256]{3,2,1,0:T(8,128)S(1)}, f32[4,1,64,256]{3,2,1,0:T(8,128)S(1)}, u32[]{:S(2)}, u32[]{:S(2)}) collective-permute-start(f32[4,1,64,256]{3,2,1,0:T(8,128)S(1)} %get-tuple-element.69), channel_id=1, source_target_pairs={{0,1},{1,2},{2,3},{3,4},{4,5},{5,6},{6,7},{7,8},{8,9},{9,10},{10,1... | collective-permute-start | bytes 786440 | tf_op jit(solution)/shard_map/ppermute | solution.py:22
  51.2 13.3 %collective-permute-start.7 = (f32[4,2,64,256]{3,2,1,0:T(8,128)S(1)}, f32[4,2,64,256]{3,2,1,0:T(8,128)S(1)}, u32[]{:S(2)}, u32[]{:S(2)}) collective-permute-start(f32[4,2,64,256]{3,2,1,0:T(8,128)S(1)} %multiply_add_fusion), channel_id=1, source_target_pairs={{0,16},{1,17},{2,18},{3,19},{4,20},{5,21},{6,22},{7,23},{8,24},{9,... | collective-permute-start | bytes 1572872 | tf_op jit(solution)/shard_map/ppermute | solution.py:31
  52.6 8.4 %collective-permute-start.10 = (f32[4,1,64,256]{3,2,1,0:T(8,128)S(1)}, f32[4,1,64,256]{3,2,1,0:T(8,128)S(1)}, u32[]{:S(2)}, u32[]{:S(2)}) collective-permute-start(f32[4,1,64,256]{3,2,1,0:T(8,128)S(1)} %get-tuple-element.46), channel_id=1, source_target_pairs={{1,0},{2,1},{3,2},{4,3},{5,4},{6,5},{7,6},{8,7},{9,8},{10,9},{11,1... | collective-permute-start | bytes 786440 | tf_op jit(solution)/shard_map/ppermute | solution.py:23
  54.0 10.1 %collective-permute-start.11 = (f32[4,1,64,256]{3,2,1,0:T(8,128)S(1)}, f32[4,1,64,256]{3,2,1,0:T(8,128)S(1)}, u32[]{:S(2)}, u32[]{:S(2)}) collective-permute-start(f32[4,1,64,256]{3,2,1,0:T(8,128)S(1)} %get-tuple-element.47), channel_id=1, source_target_pairs={{0,1},{1,2},{2,3},{3,4},{4,5},{5,6},{6,7},{7,8},{8,9},{9,10},{10,1... | collective-permute-start | bytes 786440 | tf_op jit(solution)/shard_map/ppermute | solution.py:22
  65.3 8.3 %collective-permute-start.8 = (f32[4,1,64,256]{3,2,1,0:T(8,128)S(1)}, f32[4,1,64,256]{3,2,1,0:T(8,128)S(1)}, u32[]{:S(2)}, u32[]{:S(2)}) collective-permute-start(f32[4,1,64,256]{3,2,1,0:T(8,128)S(1)} %get-tuple-element.57), channel_id=1, source_target_pairs={{1,0},{2,1},{3,2},{4,3},{5,4},{6,5},{7,6},{8,7},{9,8},{10,9},{11,1... | collective-permute-start | bytes 786440 | tf_op jit(solution)/shard_map/ppermute | solution.py:23
  68.9 10.1 %collective-permute-start.9 = (f32[4,1,64,256]{3,2,1,0:T(8,128)S(1)}, f32[4,1,64,256]{3,2,1,0:T(8,128)S(1)}, u32[]{:S(2)}, u32[]{:S(2)}) collective-permute-start(f32[4,1,64,256]{3,2,1,0:T(8,128)S(1)} %get-tuple-element.58), channel_id=1, source_target_pairs={{0,1},{1,2},{2,3},{3,4},{4,5},{5,6},{6,7},{7,8},{8,9},{9,10},{10,1... | collective-permute-start | bytes 786440 | tf_op jit(solution)/shard_map/ppermute | solution.py:22
  80.6 8.8 %collective-permute-start.12 = (f32[4,1,64,256]{3,2,1,0:T(8,128)S(1)}, f32[4,1,64,256]{3,2,1,0:T(8,128)S(1)}, u32[]{:S(2)}, u32[]{:S(2)}) collective-permute-start(f32[4,1,64,256]{3,2,1,0:T(8,128)S(1)} %get-tuple-element.35), channel_id=1, source_target_pairs={{1,0},{2,1},{3,2},{4,3},{5,4},{6,5},{7,6},{8,7},{9,8},{10,9},{11,1... | collective-permute-start | bytes 786440 | tf_op jit(solution)/shard_map/ppermute | solution.py:23
  83.4 10.0 %collective-permute-start.13 = (f32[4,1,64,256]{3,2,1,0:T(8,128)S(1)}, f32[4,1,64,256]{3,2,1,0:T(8,128)S(1)}, u32[]{:S(2)}, u32[]{:S(2)}) collective-permute-start(f32[4,1,64,256]{3,2,1,0:T(8,128)S(1)} %get-tuple-element.36), channel_id=1, source_target_pairs={{0,1},{1,2},{2,3},{3,4},{4,5},{5,6},{6,7},{7,8},{8,9},{9,10},{10,1... | collective-permute-start | bytes 786440 | tf_op jit(solution)/shard_map/ppermute | solution.py:22
where the time goes:
time: 96.7 us; the launch traced here: 95.5 us
  waiting for transfers between devices  59.6 us (62%)
  starting transfers between devices  24.2 us (25%)
  other arithmetic  8.37 us (9%)
  local copies, waits for them, and re-layouts  2.71 us (3%)
    ppermute x6, waiting for transfers between devices, padded_2(): after = lax.ppermute(first, axis, down)  34.4 us
    ppermute x6, waiting for transfers between devices, padded_2(): before = lax.ppermute(last, axis, up)  25.2 us
    ppermute x6, starting transfers between devices, padded_2(): after = lax.ppermute(first, axis, down)  19.7 us
    ppermute x2, starting transfers between devices, passed_along(): return lax.ppermute(value, axis, pairs)  3.83 us
    neg x6, other arithmetic, tendency(): advect = -(stream_speed * grad_x + center[1] * grad_y + center[2] * grad_z)  3 us
    sub x6, other arithmetic, tendency(): east_side + west_side + north_side + south_side + top_side + bottom_side  2.49 us
  transfers between devices with their start and end apart: 14, of which 12 were waited for; matrix products, arithmetic and copies ran while one was open for 3% of the time, Pallas kernels for 0%

commit v1 on v0

v1 whole, which is shorter than its diff:
```python
import functools

import jax
import jax.numpy as jnp
from jax import lax
from jax.experimental import pallas as pl
from jax.experimental.pallas import tpu as pltpu
from jax.sharding import PartitionSpec as P

ITERS = 2
GROUP = 4

time_step = 0.4
tension = 0.1
level_diffusion = 0.02
shear_rate = 1.0
half = 0.5 * time_step
MESH = pl.DeviceIdType.MESH
ROUNDS = 2 * ITERS


def swapped(p):
    return p + (p // 2) * (1 - 2 * (p % 2))


def kernel(slices, peers, init, visc_in, out, S, Yr, Ys, Q, T, N, visc,
           redist_send, redist_recv, visc_send, visc_recv, x_send, x_recv, y_send, y_recv,
           tm_send, tm_recv, out_send, out_recv):
    planes = init.shape[2]
    depth = init.shape[4]
    width, rows = S.shape[2] - 2, S.shape[3]
    t = lax.axis_index("tm")
    me = lax.axis_index("space")
    pos = lax.rem(me, GROUP)
    base = me - pos
    block = swapped(pos)
    next_group = lax.rem(me + GROUP, peers)
    prev_group = lax.rem(me + peers - GROUP, peers)
    north = base + swapped(lax.rem(block + 1, GROUP))
    south = base + swapped(lax.rem(block + GROUP - 1, GROUP))

    barrier = pltpu.get_barrier_semaphore()
    mates = [base + lax.rem(pos + k, GROUP) for k in range(1, GROUP)]
    for other in mates + [next_group, prev_group]:
        pl.semaphore_signal(barrier, inc=1, device_id=(t, other), device_id_type=MESH)

    @pl.when(t > 0)
    def _():
        pl.semaphore_signal(barrier, inc=1, device_id=(t - 1, me), device_id_type=MESH)

    @pl.when(t < slices - 1)
    def _():
        pl.semaphore_signal(barrier, inc=1, device_id=(t + 1, me), device_id_type=MESH)

    slices_near = (t > 0).astype(jnp.int32) + (t < slices - 1).astype(jnp.int32)
    pl.semaphore_wait(barrier, GROUP + 1 + slices_near)

    def remote(src, dst, send, recv, target):
        return pltpu.make_async_remote_copy(
            src_ref=src, dst_ref=dst, send_sem=send, recv_sem=recv,
            device_id=target, device_id_type=MESH)

    mine = pl.ds(1 + pos * planes, planes)
    mine_visc = pl.ds(pos * planes, planes)

    def rows_of(position):
        return pl.ds(pl.multiple_of(swapped(position) * rows, rows), rows)

    local = [
        pltpu.make_async_copy(init.at[0, :, :, rows_of(pos)], S.at[0, :, mine], redist_recv.at[0]),
        pltpu.make_async_copy(visc_in.at[:, rows_of(pos)], visc.at[mine_visc], visc_recv.at[0]),
    ]
    moved, moved_visc = [], []
    for k in (2, 1, 3):
        to = lax.rem(pos + k, GROUP)
        moved.append(remote(init.at[0, :, :, rows_of(to)], S.at[0, :, mine],
                            redist_send.at[k], redist_recv.at[k], (t, base + to)))
        moved[-1].start()
    for k in (2, 1, 3):
        to = lax.rem(pos + k, GROUP)
        moved_visc.append(remote(visc_in.at[:, rows_of(to)], visc.at[mine_visc],
                                 visc_send.at[k], visc_recv.at[k], (t, base + to)))
        moved_visc[-1].start()
    for copy in local:
        copy.start()

    shape = (rows, depth)
    row = lax.broadcasted_iota(jnp.int32, shape, 0)
    lane = lax.broadcasted_iota(jnp.int32, shape, 1)
    half_shear = 0.5 * (shear_rate * (lane.astype(jnp.float32) + 0.5) / depth)

    def tendency(r, x):
        diffs, laps, centers = [], [], []
        for k in range(4):
            c, e, w = S[r, k, x + 1], S[r, k, x + 2], S[r, k, x]
            n = jnp.where(row == rows - 1, Yr[r, 1, k, x], pltpu.roll(c, rows - 1, 0))
            s = jnp.where(row == 0, Yr[r, 0, k, x], pltpu.roll(c, 1, 0))
            a = jnp.where(lane == depth - 1, 0.0, pltpu.roll(c, depth - 1, 1))
            b = jnp.where(lane == 0, 0.0, pltpu.roll(c, 1, 1))
            diffs.append((e - w, n - s, a - b))
            laps.append(((e + w) + (n + s)) + (a + b) - 6.0 * c)
            centers.append(c)
        su = 0.5 * centers[0] + half_shear
        sv, sw = 0.5 * centers[1], 0.5 * centers[2]
        mu = visc[x]
        curve = (0.5 * tension) * laps[3]
        res = []
        for k in range(4):
            dx, dy, dz = diffs[k]
            adv = -(su * dx + sv * dy + sw * dz)
            if k < 3:
                res.append(adv + mu * laps[k] + curve * diffs[3][k])
            else:
                res.append(adv + level_diffusion * laps[3])
        return res

    def pack(r, x, k, value):
        Ys[r, 0, k, x] = value[0:1]
        Ys[r, 1, k, x] = value[rows - 1:rows]

    def put(r, x, k, value):
        S[r, k, x + 1] = value
        pack(r, x, k, value)

    def x_copies(r):
        return [
            remote(S.at[r, :, pl.ds(width, 1)], S.at[r, :, pl.ds(0, 1)],
                   x_send.at[r, 0], x_recv.at[r, 0], (t, next_group)),
            remote(S.at[r, :, pl.ds(1, 1)], S.at[r, :, pl.ds(width + 1, 1)],
                   x_send.at[r, 1], x_recv.at[r, 1], (t, prev_group)),
        ]

    def y_copies(r):
        return [
            remote(Ys.at[r, 1], Yr.at[r, 0], y_send.at[r, 0], y_recv.at[r, 0], (t, north)),
            remote(Ys.at[r, 0], Yr.at[r, 1], y_send.at[r, 1], y_recv.at[r, 1], (t, south)),
        ]

    def start(copies):
        for copy in copies:
            copy.start()

    def over(lo, hi, body):
        def step(x, carry):
            body(x)
            return carry
        lax.fori_loop(lo, hi, step, 0)

    def edges_first(body, after_edges):
        over(0, 1, body)
        over(width - 1, width, body)
        after_edges()
        over(1, width - 1, body)

    def interior_first(r, body):
        for copy in y_copies(r):
            copy.wait_recv()
        over(1, width - 1, body)
        for copy in x_copies(r):
            copy.wait_recv()
        over(0, 1, body)
        over(width - 1, width, body)

    def passed(index, src):
        copy = remote(src, Q.at[index], tm_send.at[index], tm_recv.at[index], (t + 1, me))

        @pl.when(t < slices - 1)
        def _():
            copy.start()

    def own(index, src):
        @pl.when(t == 0)
        def _():
            pltpu.make_async_copy(src, Q.at[index], tm_recv.at[index]).start()

    def arrived(index):
        pltpu.make_async_copy(Q.at[index], Q.at[index], tm_recv.at[index]).wait()

    for copy in local + moved:
        if copy is local[1]:
            continue
        if copy is local[0]:
            copy.wait()
        else:
            copy.wait_recv()
    start(x_copies(0))

    def pack_first(x):
        for k in range(4):
            pack(0, x, k, S[0, k, x + 1])

    over(0, width, pack_first)
    start(y_copies(0))
    center = S.at[0, :, pl.ds(1, width)]
    passed(0, center)
    own(0, center)
    local[1].wait()
    for copy in moved_visc:
        copy.wait_recv()

    def first(x):
        for k, f in enumerate(tendency(0, x)):
            T[0, k, x] = f

    interior_first(0, first)
    passed(1, T.at[0])
    own(1, T.at[0])

    arrived(0)
    arrived(1)

    def start_zero(x):
        for k in range(4):
            g = T[0, k, x]
            put(1, x, k, Q[0, k, x] + half * (Q[1, k, x] - g)
                + time_step * (5.0 / 24.0 * g + 1.0 / 3.0 * g - 1.0 / 24.0 * g))

    edges_first(start_zero, lambda: start(x_copies(1)))
    start(y_copies(1))

    def middle_zero(x):
        for k, f in enumerate(tendency(1, x)):
            g = T[0, k, x]
            T[1, k, x] = f
            put(2, x, k, S[1, k, x + 1] + half * (f - g)
                + time_step * (-1.0 / 24.0 * g + 1.0 / 3.0 * g + 5.0 / 24.0 * g))

    interior_first(1, middle_zero)
    start(x_copies(2))
    start(y_copies(2))

    def last_zero(x):
        for k, f in enumerate(tendency(2, x)):
            T[2, k, x] = f
            N[k, x] = S[2, k, x + 1] + half * f

    interior_first(2, last_zero)
    passed(2, N)

    @pl.when(t == 0)
    def _():
        def keep(x):
            for k in range(4):
                Q[2, k, x] = Q[0, k, x] + half * Q[1, k, x]
        over(0, width, keep)

    @pl.when(t > 0)
    def _():
        arrived(2)

    def start_one(x):
        for k in range(4):
            g = Q[1, k, x]
            put(3, x, k, Q[2, k, x] - half * g
                + time_step * (5.0 / 24.0 * g + 1.0 / 3.0 * T[1, k, x] - 1.0 / 24.0 * T[2, k, x]))

    edges_first(start_one, lambda: start(x_copies(3)))
    start(y_copies(3))
    for copy in y_copies(3) + x_copies(3):
        copy.wait_recv()

    def middle_one(x):
        for k, f in enumerate(tendency(3, x)):
            T[3, k, x] = (S[3, k, x + 1] + half * (f - T[1, k, x])
                          + time_step * (-1.0 / 24.0 * Q[1, k, x] + 1.0 / 3.0 * T[1, k, x]
                                         + 5.0 / 24.0 * T[2, k, x]))

    back = []
    own_rows = rows_of(pos)
    for k in (2, 1, 3, 0):
        to = lax.rem(pos + k, GROUP)
        over(to * planes, (to + 1) * planes, middle_one)
        src = T.at[3, :, pl.ds(to * planes, planes)]
        dst = out.at[0, :, :, own_rows]
        if k:
            back.append(remote(src, dst, out_send.at[k], out_recv.at[k], (t, base + to)))
        else:
            back.append(pltpu.make_async_copy(src, dst, out_recv.at[0]))
        back[-1].start()
    for copy in moved + moved_visc:
        copy.wait_send()
    for r in range(ROUNDS):
        for copy in x_copies(r) + y_copies(r):
            copy.wait_send()

    @pl.when(t < slices - 1)
    def _():
        for index, src in ((0, center), (1, T.at[0]), (2, N)):
            remote(src, Q.at[index], tm_send.at[index], tm_recv.at[index], (t + 1, me)).wait_send()

    for copy in back[:3]:
        copy.wait_recv()
        copy.wait_send()
    back[3].wait()


def on_device(slices, peers, initial_guess, viscosity):
    _, comps, planes, ny, nz = initial_guess.shape
    width, rows = planes * GROUP, ny // GROUP
    f32 = jnp.float32
    dma = pltpu.SemaphoreType.DMA
    return pl.pallas_call(
        functools.partial(kernel, slices, peers),
        out_shape=jax.ShapeDtypeStruct(initial_guess.shape, f32),
        in_specs=[pl.BlockSpec(memory_space=pl.ANY)] * 2,
        out_specs=pl.BlockSpec(memory_space=pl.ANY),
        scratch_shapes=[
            pltpu.VMEM((ROUNDS, comps, width + 2, rows, nz), f32),
            pltpu.VMEM((ROUNDS, 2, comps, width, 1, nz), f32),
            pltpu.VMEM((ROUNDS, 2, comps, width, 1, nz), f32),
            pltpu.VMEM((3, comps, width, rows, nz), f32),
            pltpu.VMEM((4, comps, width, rows, nz), f32),
            pltpu.VMEM((comps, width, rows, nz), f32),
            pltpu.VMEM((width, rows, nz), f32),
            dma((GROUP,)), dma((GROUP,)), dma((GROUP,)), dma((GROUP,)),
            dma((ROUNDS, 2)), dma((ROUNDS, 2)), dma((ROUNDS, 2)), dma((ROUNDS, 2)),
            dma((3,)), dma((3,)), dma((GROUP,)), dma((GROUP,)),
        ],
        compiler_params=pltpu.CompilerParams(
            collective_id=0, has_side_effects=True, vmem_limit_bytes=40 * 1024 * 1024
        ),
    )(initial_guess, viscosity)


def solution(mesh):
    return jax.shard_map(
        functools.partial(on_device, mesh.shape["tm"], mesh.shape["space"]),
        mesh=mesh,
        in_specs=(P("tm", None, "space", None, None), P("space", None, None)),
        out_specs=P("tm", None, "space", None, None),
        check_vma=False,
    )
```

time: 96.7 us -> 45.7 us (0.47); the launches traced: 95.5 us -> 45.6 us
  waiting for transfers between devices: 59.6 us -> 0 us
  Pallas kernels: 0 us -> 42.8 us
  starting transfers between devices: 24.2 us -> 0 us
  other arithmetic: 8.37 us -> 0 us
    ppermute x14 -> x0, waiting for transfers between devices: 59.6 us -> none  [the longest x6 34.4 us: padded_2(): after = lax.ppermute(first, axis, down)]
    pallas_call x0 -> x1, Pallas kernels: none -> 42.8 us  [on_device(): pl.pallas_call(functools.partial(kernel, slices, peers), out_shape=jax.Sh...]
    ppermute x14 -> x0, starting transfers between devices: 24.2 us -> none  [the longest x6 19.7 us: padded_2(): after = lax.ppermute(first, axis, down)]
    neg x6 -> x0, other arithmetic: 3 us -> none  [tendency(): advect = -(stream_speed * grad_x + center[1] * grad_y + center[2] * grad_z)]
    sub x6 -> x0, other arithmetic: 2.49 us -> none  [tendency(): east_side + west_side + north_side + south_side + top_side + bottom_side]
    unnamed x4 -> x5, local copies, waits for them, and re-layouts: 0.86 us -> 2.74 us
    slice x18 -> x0, local copies, waits for them, and re-layouts: 1.85 us -> none  [the longest x6 1.26 us: padded_2(): first = lax.slice_in_dim(value, 0, width, axis=dim)]
    add x7 -> x0, other arithmetic: 1.16 us -> none  [the longest x4 0.59 us: tendency(): advect[:3] + viscosity * laplace[:3]]
  transfers between devices with their start and end apart: 14 -> 0, of which waited for: 12 -> 0; matrix products, arithmetic and copies ran while one was open for 3% -> 0% of each run, Pallas kernels for 0% -> 0%
where the time goes in v1:
time: 45.7 us; the launch traced here: 45.6 us
  Pallas kernels  42.8 us (94%)
  local copies, waits for them, and re-layouts  2.74 us (6%)
    pallas_call x1, Pallas kernels, on_device(): pl.pallas_call(functools.partial(kernel, slices, peers), out_shape=jax.Sh...  42.8 us
    unnamed x5, local copies, waits for them, and re-layouts  2.74 us

profile of v1, /device:TPU:0, one launch (start us, length us, event | category | flops | bytes accessed | tf_op | source)
XLA Modules:
  0.0 45.6 jit_solution(4852114204768756553)
XLA Ops:
  0.0 0.0 copy-start
  0.0 1.0 %copy-done = f32[1,4,2,64,256]{4,3,2,1,0:T(8,128)S(1)} copy-done((f32[1,4,2,64,256]{4,3,2,1,0:T(8,128)S(1)}, f32[1,4,2,64,256]{4,3,2,1,0:T(8,128)}, u32[]{:S(2)}) %copy-start) | copy-done | bytes 524312
  1.0 0.0 copy-start.1
  1.0 0.9 %copy-done.1 = f32[2,64,256]{2,1,0:T(8,128)S(1)} copy-done((f32[2,64,256]{2,1,0:T(8,128)S(1)}, f32[2,64,256]{2,1,0:T(8,128)}, u32[]{:S(2)}) %copy-start.1) | copy-done | bytes 131096
  1.9 42.8 %shard_map.28 = f32[1,4,2,64,256]{4,3,2,1,0:T(8,128)S(1)} custom-call(f32[1,4,2,64,256]{4,3,2,1,0:T(8,128)S(1)} %copy-done, f32[2,64,256]{2,1,0:T(8,128)S(1)} %copy-done.1), custom_call_target="tpu_custom_call" | custom-call | tf_op jit(solution)/shard_map/pallas_call | solution.py:302
  44.8 0.8 %copy.4 = f32[1,4,2,64,256]{4,3,2,1,0:T(8,128)} copy(f32[1,4,2,64,256]{4,3,2,1,0:T(8,128)S(1)} %shard_map.28) | data formatting | bytes 1048576
Async XLA Ops:
  0.0 1.0 %copy-start = (f32[1,4,2,64,256]{4,3,2,1,0:T(8,128)S(1)}, f32[1,4,2,64,256]{4,3,2,1,0:T(8,128)}, u32[]{:S(2)}) copy-start(f32[1,4,2,64,256]{4,3,2,1,0:T(8,128)} %init.1) | copy-start | bytes 1572868
  1.0 0.9 %copy-start.1 = (f32[2,64,256]{2,1,0:T(8,128)S(1)}, f32[2,64,256]{2,1,0:T(8,128)}, u32[]{:S(2)}) copy-start(f32[2,64,256]{2,1,0:T(8,128)} %visc_in.1) | copy-start | bytes 393220

commit v2 on v1

--- a/solution.py
+++ b/solution.py
@@ -25,7 +25,7 @@
 
 def kernel(slices, peers, init, visc_in, out, S, Yr, Ys, Q, T, N, visc,
            redist_send, redist_recv, visc_send, visc_recv, x_send, x_recv, y_send, y_recv,
-           tm_send, tm_recv, out_send, out_recv):
+           edge_send, tm_send, tm_recv, out_send, out_recv):
     planes = init.shape[2]
     depth = init.shape[4]
     width, rows = S.shape[2] - 2, S.shape[3]
@@ -80,7 +80,6 @@
         to = lax.rem(pos + k, GROUP)
         moved_visc.append(remote(visc_in.at[:, rows_of(to)], visc.at[mine_visc],
                                  visc_send.at[k], visc_recv.at[k], (t, base + to)))
-        moved_visc[-1].start()
     for copy in local:
         copy.start()
 
@@ -152,29 +151,39 @@
         after_edges()
         over(1, width - 1, body)
 
-    def interior_first(r, body):
+    def interior_first(r, body, between=lambda: None):
         for copy in y_copies(r):
             copy.wait_recv()
         over(1, width - 1, body)
+        between()
         for copy in x_copies(r):
             copy.wait_recv()
         over(0, 1, body)
         over(width - 1, width, body)
 
-    def passed(index, src):
-        copy = remote(src, Q.at[index], tm_send.at[index], tm_recv.at[index], (t + 1, me))
-
+    parts = ((0, width),)
+
+    def to_next(index, part, src):
+        at = pl.ds(*(parts[part] if index else (0, width)))
+        return remote(src.at[:, at], Q.at[index, :, at], tm_send.at[index, part],
+                      tm_recv.at[index, part], (t + 1, me))
+
+    def passed(index, part, src):
         @pl.when(t < slices - 1)
         def _():
-            copy.start()
-
-    def own(index, src):
+            to_next(index, part, src).start()
+
+    def own(index, part, src):
+        at = pl.ds(*(parts[part] if index else (0, width)))
+
         @pl.when(t == 0)
         def _():
-            pltpu.make_async_copy(src, Q.at[index], tm_recv.at[index]).start()
-
-    def arrived(index):
-        pltpu.make_async_copy(Q.at[index], Q.at[index], tm_recv.at[index]).wait()
+            pltpu.make_async_copy(src.at[:, at], Q.at[index, :, at], tm_recv.at[index, part]).start()
+
+    def arrived(index, part):
+        at = pl.ds(*(parts[part] if index else (0, width)))
+        block_in = Q.at[index, :, at]
+        pltpu.make_async_copy(block_in, block_in, tm_recv.at[index, part]).wait()
 
     for copy in local + moved:
         if copy is local[1]:
@@ -184,6 +193,7 @@
         else:
             copy.wait_recv()
     start(x_copies(0))
+    start(moved_visc)
 
     def pack_first(x):
         for k in range(4):
@@ -192,8 +202,8 @@
     over(0, width, pack_first)
     start(y_copies(0))
     center = S.at[0, :, pl.ds(1, width)]
-    passed(0, center)
-    own(0, center)
+    passed(0, 0, center)
+    own(0, 0, center)
     local[1].wait()
     for copy in moved_visc:
         copy.wait_recv()
@@ -202,12 +212,16 @@
         for k, f in enumerate(tendency(0, x)):
             T[0, k, x] = f
 
+    def first_part(part):
+        passed(1, part, T.at[0])
+        own(1, part, T.at[0])
+
     interior_first(0, first)
-    passed(1, T.at[0])
-    own(1, T.at[0])
-
-    arrived(0)
-    arrived(1)
+    first_part(0)
+
+    arrived(0, 0)
+    for part in range(1):
+        arrived(1, part)
 
     def start_zero(x):
         for k in range(4):
@@ -235,7 +249,7 @@
             N[k, x] = S[2, k, x + 1] + half * f
 
     interior_first(2, last_zero)
-    passed(2, N)
+    passed(2, 0, N)
 
     @pl.when(t == 0)
     def _():
@@ -246,7 +260,8 @@
 
     @pl.when(t > 0)
     def _():
-        arrived(2)
+        for part in range(1):
+            arrived(2, part)
 
     def start_one(x):
         for k in range(4):
@@ -256,7 +271,7 @@
 
     edges_first(start_one, lambda: start(x_copies(3)))
     start(y_copies(3))
-    for copy in y_copies(3) + x_copies(3):
+    for copy in y_copies(3):
         copy.wait_recv()
 
     def middle_one(x):
@@ -265,18 +280,28 @@
                           + time_step * (-1.0 / 24.0 * Q[1, k, x] + 1.0 / 3.0 * T[1, k, x]
                                          + 5.0 / 24.0 * T[2, k, x]))
 
-    back = []
-    own_rows = rows_of(pos)
-    for k in (2, 1, 3, 0):
-        to = lax.rem(pos + k, GROUP)
+    def back(to):
+        return (T.at[3, :, pl.ds(to * planes, planes)], out.at[0, :, :, rows_of(pos)])
+
+    def gone(to):
+        k = lax.rem(to - pos + GROUP, GROUP)
+        return remote(*back(to), out_send.at[k], out_recv.at[k], (t, base + to))
+
+    order = list(range(1, GROUP - 1)) + [0, GROUP - 1]
+    for to in order:
+        if to == 0:
+            for copy in x_copies(3):
+                copy.wait_recv()
         over(to * planes, (to + 1) * planes, middle_one)
-        src = T.at[3, :, pl.ds(to * planes, planes)]
-        dst = out.at[0, :, :, own_rows]
-        if k:
-            back.append(remote(src, dst, out_send.at[k], out_recv.at[k], (t, base + to)))
-        else:
-            back.append(pltpu.make_async_copy(src, dst, out_recv.at[0]))
-        back[-1].start()
+
+        @pl.when(pos == to)
+        def _():
+            pltpu.make_async_copy(*back(to), out_recv.at[0]).start()
+
+        @pl.when(pos != to)
+        def _():
+            gone(to).start()
+
     for copy in moved + moved_visc:
         copy.wait_send()
     for r in range(ROUNDS):
@@ -285,13 +310,18 @@
 
     @pl.when(t < slices - 1)
     def _():
-        for index, src in ((0, center), (1, T.at[0]), (2, N)):
-            remote(src, Q.at[index], tm_send.at[index], tm_recv.at[index], (t + 1, me)).wait_send()
-
-    for copy in back[:3]:
-        copy.wait_recv()
-        copy.wait_send()
-    back[3].wait()
+        to_next(0, 0, center).wait_send()
+        for part in range(1):
+            to_next(1, part, T.at[0]).wait_send()
+            to_next(2, part, N).wait_send()
+
+    for to in order:
+        @pl.when(pos != to)
+        def _():
+            gone(to).wait_send()
+
+    for k in range(GROUP):
+        pltpu.make_async_copy(*back(0), out_recv.at[k]).wait()
 
 
 def on_device(slices, peers, initial_guess, viscosity):
@@ -314,10 +344,10 @@
             pltpu.VMEM((width, rows, nz), f32),
             dma((GROUP,)), dma((GROUP,)), dma((GROUP,)), dma((GROUP,)),
             dma((ROUNDS, 2)), dma((ROUNDS, 2)), dma((ROUNDS, 2)), dma((ROUNDS, 2)),
-            dma((3,)), dma((3,)), dma((GROUP,)), dma((GROUP,)),
+            dma((2, GROUP)), dma((3, 3)), dma((3, 3)), dma((GROUP,)), dma((GROUP,)),
         ],
         compiler_params=pltpu.CompilerParams(
-            collective_id=0, has_side_effects=True, vmem_limit_bytes=40 * 1024 * 1024
+            collective_id=0, has_side_effects=True, vmem_limit_bytes=62 * 1024 * 1024
         ),
     )(initial_guess, viscosity)
 

time: 45.7 us -> 44.1 us (0.965)
  local copies, waits for them, and re-layouts: 2.74 us -> 1.87 us
  Pallas kernels: 42.8 us -> 42.1 us
    unnamed x5 -> x1, local copies, waits for them, and re-layouts: 2.74 us -> 1.87 us
    pallas_call x1, Pallas kernels: 42.8 us -> 42.1 us  [on_device(): pl.pallas_call(functools.partial(kernel, slices, peers), out_shape=jax.Sh...]
where the time goes in v2:
time: 44.1 us; the launch traced here: 43.9 us
  Pallas kernels  42.1 us (95%)
  local copies, waits for them, and re-layouts  1.87 us (4%)
    pallas_call x1, Pallas kernels, on_device(): pl.pallas_call(functools.partial(kernel, slices, peers), out_shape=jax.Sh...  42.1 us
    unnamed x1, local copies, waits for them, and re-layouts  1.87 us

profile of v2, /device:TPU:0, one launch (start us, length us, event | category | flops | bytes accessed | tf_op | source)
XLA Modules:
  0.0 43.9 jit_solution(9275555595252921778)
XLA Ops:
  0.0 42.1 %shard_map.28 = f32[1,4,2,64,256]{4,3,2,1,0:T(8,128)} custom-call(f32[1,4,2,64,256]{4,3,2,1,0:T(8,128)} %init.1, f32[2,64,256]{2,1,0:T(8,128)} %visc_in.1), custom_call_target="tpu_custom_call" | custom-call | tf_op jit(solution)/shard_map/pallas_call | solution.py:332
  42.1 1.9 %copy.4 = f32[1,4,2,64,256]{4,3,2,1,0:T(8,128)} copy(f32[1,4,2,64,256]{4,3,2,1,0:T(8,128)} %shard_map.28) | data formatting | bytes 1048576

commit v3 on v2

--- a/solution.py
+++ b/solution.py
@@ -39,6 +39,16 @@
     north = base + swapped(lax.rem(block + 1, GROUP))
     south = base + swapped(lax.rem(block + GROUP - 1, GROUP))
 
+    mine = pl.ds(1 + pos * planes, planes)
+    mine_visc = pl.ds(pos * planes, planes)
+
+    def rows_of(position):
+        return pl.ds(pl.multiple_of(swapped(position) * rows, rows), rows)
+
+    local = [
+        pltpu.make_async_copy(init.at[0, :, :, rows_of(pos)], S.at[0, :, mine], redist_recv.at[0]),
+        pltpu.make_async_copy(visc_in.at[:, rows_of(pos)], visc.at[mine_visc], visc_recv.at[0]),
+    ]
     barrier = pltpu.get_barrier_semaphore()
     mates = [base + lax.rem(pos + k, GROUP) for k in range(1, GROUP)]
     for other in mates + [next_group, prev_group]:
@@ -52,6 +62,8 @@
     def _():
         pl.semaphore_signal(barrier, inc=1, device_id=(t + 1, me), device_id_type=MESH)
 
+    for copy in local:
+        copy.start()
     slices_near = (t > 0).astype(jnp.int32) + (t < slices - 1).astype(jnp.int32)
     pl.semaphore_wait(barrier, GROUP + 1 + slices_near)
 
@@ -60,28 +72,16 @@
             src_ref=src, dst_ref=dst, send_sem=send, recv_sem=recv,
             device_id=target, device_id_type=MESH)
 
-    mine = pl.ds(1 + pos * planes, planes)
-    mine_visc = pl.ds(pos * planes, planes)
-
-    def rows_of(position):
-        return pl.ds(pl.multiple_of(swapped(position) * rows, rows), rows)
-
-    local = [
-        pltpu.make_async_copy(init.at[0, :, :, rows_of(pos)], S.at[0, :, mine], redist_recv.at[0]),
-        pltpu.make_async_copy(visc_in.at[:, rows_of(pos)], visc.at[mine_visc], visc_recv.at[0]),
-    ]
     moved, moved_visc = [], []
-    for k in (2, 1, 3):
+    for k in (1, 3, 2):
         to = lax.rem(pos + k, GROUP)
         moved.append(remote(init.at[0, :, :, rows_of(to)], S.at[0, :, mine],
                             redist_send.at[k], redist_recv.at[k], (t, base + to)))
         moved[-1].start()
-    for k in (2, 1, 3):
+    for k in (1, 3, 2):
         to = lax.rem(pos + k, GROUP)
         moved_visc.append(remote(visc_in.at[:, rows_of(to)], visc.at[mine_visc],
                                  visc_send.at[k], visc_recv.at[k], (t, base + to)))
-    for copy in local:
-        copy.start()
 
     shape = (rows, depth)
     row = lax.broadcasted_iota(jnp.int32, shape, 0)

time: 44.1 us -> 44.1 us (level)
  no operation moved by 1% of the time
where the time goes in v3:
time: 44.1 us; the launch traced here: 43.9 us
  Pallas kernels  42.1 us (95%)
  local copies, waits for them, and re-layouts  1.87 us (4%)
    pallas_call x1, Pallas kernels, on_device(): pl.pallas_call(functools.partial(kernel, slices, peers), out_shape=jax.Sh...  42.1 us
    unnamed x1, local copies, waits for them, and re-layouts  1.87 us

profile of v3, /device:TPU:0, one launch (start us, length us, event | category | flops | bytes accessed | tf_op | source)
XLA Modules:
  0.0 43.9 jit_solution(3329762370537443297)
XLA Ops:
  0.0 42.1 %shard_map.28 = f32[1,4,2,64,256]{4,3,2,1,0:T(8,128)} custom-call(f32[1,4,2,64,256]{4,3,2,1,0:T(8,128)} %init.1, f32[2,64,256]{2,1,0:T(8,128)} %visc_in.1), custom_call_target="tpu_custom_call" | custom-call | tf_op jit(solution)/shard_map/pallas_call | solution.py:332
  42.1 1.9 %copy.4 = f32[1,4,2,64,256]{4,3,2,1,0:T(8,128)} copy(f32[1,4,2,64,256]{4,3,2,1,0:T(8,128)} %shard_map.28) | data formatting | bytes 1048576
